TPU v7x, 32 devices: a whole 2x2x4 slice. The times are simulated.
32 devices in a mesh: clips: 2 (over y), tm: 4 (over z), height: 4 (over x, core).
Axes of the slice: x: 2, y: 2, z: 4, core: 2. Of those that a mesh axis runs over, the one named last changes fastest.
Arguments:
- clip_frames: bfloat16 [32, 32, 16, 192], P(('clips', 'tm'), 'height'), parts along dimension 0, may hold values from -6 to 6
- w_first: bfloat16 [3, 3, 3, 192, 192], replicated, may hold values from -0.078125 to 0.078125
- b_first: float32 [192], replicated, may hold values from -3 to 3
- w_second: bfloat16 [3, 3, 3, 192, 192], replicated, may hold values from -0.078125 to 0.078125
- b_second: float32 [192], replicated, may hold values from -3 to 3
Outputs:
- block_out: bfloat16 [32, 32, 16, 192], P(('clips', 'tm'), 'height'), parts along dimension 0
There are 2 independent parts, one for each index of `clips`. A program takes and returns all parts, laid end to end along the dimension named above; an argument that names none is the same for every part. Nothing has to cross between parts.
All inputs are finite; a program needn't handle non-finite values.
Results may differ from a plain program's by a relative error of at most 0.003.
Values may be sent and summed in bfloat16 or wider, within the bound.
A program may use at most 64 MiB of HBM per device.

v0:
```python
import jax
import jax.numpy as jnp
from jax import lax
from jax.sharding import PartitionSpec as P


def shifted(value, axis, steps):
    count = lax.axis_size(axis)
    leading, last = (max(0, -steps), min(count, count - steps))
    return lax.ppermute(value, axis, [(source, source + steps) for source in range(leading, last)])


def with_halo(value, sides, width):
    for axis, dim in sides:
        peers, length = (lax.axis_size(axis), value.shape[dim])
        up = [(i, (i + 1) % peers) for i in range(peers - 1)]
        down = [(j, i) for i, j in up]
        last = lax.slice_in_dim(value, length - width, length, axis=dim)
        leading = lax.slice_in_dim(value, 0, width, axis=dim)
        before = lax.ppermute(last, axis, up)
        after = lax.ppermute(leading, axis, down)
        value = jnp.concatenate([before, value, after], axis=dim)
    return value


def conv_valid(padded, weight):
    frame_count = padded.shape[0] - 2
    row_count = padded.shape[1] - 2
    col_count = padded.shape[2] - 2
    chans = weight.shape[3]
    summed = jnp.zeros((frame_count * row_count * col_count, weight.shape[4]), jnp.float32)
    for tap_time in range(3):
        stacked = jnp.concatenate(
            [
                padded[
                    tap_time : tap_time + frame_count,
                    tap_row : tap_row + row_count,
                    tap_col : tap_col + col_count,
                ]
                for tap_row in range(3)
                for tap_col in range(3)
            ],
            -1,
        )
        stacked = stacked.reshape(-1, 9 * chans)
        kernel = weight[tap_time].reshape(9 * chans, weight.shape[4])
        summed = summed + jnp.dot(stacked, kernel, preferred_element_type=jnp.float32)
    return summed.reshape(frame_count, row_count, col_count, weight.shape[4])


def pad_columns(field):
    return jnp.pad(field, ((0, 0), (0, 0), (1, 1), (0, 0)))


def context(field):
    last_frames = field[field.shape[0] - 2 :]
    earlier = shifted(last_frames, "tm", 1)
    extended = jnp.concatenate([earlier, field], 0)
    extended = with_halo(extended, (("height", 1),), 1)
    return pad_columns(extended)


def local(clip_frames, w_first, b_first, w_second, b_second):
    activated = jax.nn.silu(clip_frames.astype(jnp.float32)).astype(jnp.bfloat16)
    hidden = conv_valid(context(activated), w_first) + b_first
    gated = jax.nn.silu(hidden).astype(jnp.bfloat16)
    second = conv_valid(context(gated), w_second)
    return (clip_frames.astype(jnp.float32) + second + b_second).astype(jnp.bfloat16)


def solution(mesh):
    return jax.shard_map(
        local,
        mesh=mesh,
        in_specs=(P(("clips", "tm"), "height", None, None), P(), P(), P(), P()),
        out_specs=P(("clips", "tm"), "height", None, None),
        check_vma=False,
    )
```

profile of v0, /device:TPU:1, one launch (start us, length us, event | category | flops | bytes accessed | tf_op | source)
XLA Modules:
  0.0 68.7 jit_solution(13731439555836463821)
XLA Ops:
  0.0 1.1 %fusion.14 = bf16[4,8,16,192]{3,2,1,0:T(8,128)(2,1)S(1)} fusion(bf16[4,8,16,192]{3,2,1,0:T(8,128)(2,1)} %param.5), kind=kLoop, calls=%fused_computation.25 | loop fusion | flops 589824 | bytes 393216 | tf_op jit(solution)/shard_map/convert_element_type | solution.py:64
  1.1 4.0 %collective-permute-start = (bf16[2,8,16,192]{3,2,1,0:T(8,128)(2,1)S(1)}, bf16[2,8,16,192]{3,2,1,0:T(8,128)(2,1)S(1)}, u32[]{:S(2)}, u32[]{:S(2)}) collective-permute-start(bf16[2,8,16,192]{3,2,1,0:T(8,128)(2,1)S(1)} %slice.294), channel_id=1, source_target_pairs={{0,4},{4,8},{8,12},{1,5},{5,9},{9,13},{2,6},{6,10},{10,14},{3,7},{... | collective-permute-start | bytes 294920 | tf_op jit(solution)/shard_map/ppermute | solution.py:10
  5.2 3.2 %fusion.20 = (bf16[1,3,3,192,192]{4,3,2,1,0:T(8,128)(2,1)}, bf16[1,3,3,192,192]{4,3,2,1,0:T(8,128)(2,1)S(1)}, bf16[1,3,3,192,192]{4,3,2,1,0:T(8,128)(2,1)}) fusion(bf16[3,3,3,192,192]{4,3,2,1,0:T(8,128)(2,1)} %param.6), kind=kLoop, calls=%fused_computation.46 | loop fusion | bytes 3981312 | tf_op jit(solution)/shard_map/slice | solution.py:46
  8.3 0.0 collective-permute-done
  8.4 4.0 %collective-permute-start.1 = (bf16[6,1,16,192]{3,2,1,0:T(8,128)(2,1)S(1)}, bf16[6,1,16,192]{3,2,1,0:T(8,128)(2,1)S(1)}, u32[]{:S(2)}, u32[]{:S(2)}) collective-permute-start(bf16[6,1,16,192]{3,2,1,0:T(8,128)(2,1)S(1)} %get-tuple-element.69), channel_id=1, source_target_pairs={{0,1},{1,2},{2,3},{4,5},{5,6},{6,7},{8,9},{9,10},{10,11},{12,13},{... | collective-permute-start | bytes 110600 | tf_op jit(solution)/shard_map/ppermute | solution.py:20
  12.3 1.9 %collective-permute-start.2 = (bf16[6,1,16,192]{3,2,1,0:T(8,128)(2,1)S(1)}, bf16[6,1,16,192]{3,2,1,0:T(8,128)(2,1)S(1)}, u32[]{:S(2)}, u32[]{:S(2)}) collective-permute-start(bf16[6,1,16,192]{3,2,1,0:T(8,128)(2,1)S(1)} %get-tuple-element.70), channel_id=1, source_target_pairs={{1,0},{2,1},{3,2},{5,4},{6,5},{7,6},{9,8},{10,9},{11,10},{13,12},{... | collective-permute-start | bytes 110600 | tf_op jit(solution)/shard_map/ppermute | solution.py:21
  14.3 0.8 %pad_maximum_fusion.3 = (bf16[4,8,16,192]{3,2,1,0:T(8,128)(2,1)}, bf16[4,8,16,192]{3,2,1,0:T(8,128)(2,1)S(1)}) fusion(bf16[4,8,16,192]{3,2,1,0:T(8,128)(2,1)S(1)} %fusion.14, bf16[2,8,16,192]{3,2,1,0:T(8,128)(2,1)S(1)} %collective-permute-done), kind=kLoop, calls=%fused_computation.40 | loop fusion | flops 196608 | bytes 688128 | tf_op jit(solution)/shard_map/concatenate | solution.py:58
  15.1 0.0 collective-permute-done.1
  15.1 2.7 %collective-permute-done.2 = bf16[6,1,16,192]{3,2,1,0:T(8,128)(2,1)S(1)} collective-permute-done((bf16[6,1,16,192]{3,2,1,0:T(8,128)(2,1)S(1)}, bf16[6,1,16,192]{3,2,1,0:T(8,128)(2,1)S(1)}, u32[]{:S(2)}, u32[]{:S(2)}) %collective-permute-start.2) | collective-permute-done | bytes 36896 | tf_op jit(solution)/shard_map/ppermute | solution.py:21
  17.8 0.4 fusion.8
  18.1 2.2 %fusion.22 = (bf16[4,8,16,192]{3,2,1,0:T(8,128)(2,1)}, bf16[4,8,16,192]{3,2,1,0:T(8,128)(2,1)}, bf16[4,8,16,192]{3,2,1,0:T(8,128)(2,1)}, bf16[4,8,16,192]{3,2,1,...) fusion(bf16[6,10,18,192]{3,2,1,0:T(8,128)(2,1)S(1)} %fusion.8), kind=kLoop, calls=%fused_computation.48 | loop fusion | bytes 7077888 | tf_op jit(solution)/shard_map/slice | solution.py:35
  20.4 0.2 pad_maximum_fusion
  20.6 1.2 %fusion.25 = (bf16[4,8,16,192]{3,2,1,0:T(8,128)(2,1)}, bf16[4,8,16,192]{3,2,1,0:T(8,128)(2,1)}, bf16[4,8,16,192]{3,2,1,0:T(8,128)(2,1)}, bf16[4,8,16,192]{3,2,1,...) fusion(bf16[6,9,16,192]{3,2,1,0:T(8,128)(2,1)S(1)} %get-tuple-element.67, ...), kind=kLoop, calls=%fused_computation.51 | loop fusion | bytes 2359296 | tf_op jit(solution)/shard_map/slice | solution.py:35
  21.8 2.8 %concatenate.54 = bf16[4,8,16,1728]{3,2,1,0:T(8,128)(2,1)S(1)} concatenate(bf16[4,8,16,192]{3,2,1,0:T(8,128)(2,1)} %get-tuple-element.46, bf16[4,8,16,192]{3,2,1,0:T(8,128)(2,1)} %get-tuple-element.71, bf16[4,8,16,192]{3,2,1,0:T(8,128)(2,1)} %get-tuple-element.45, bf16[4,8,16,192]{3,2,1,0:T(8,128)(2,1)} %get-tuple-element.44, bf16[4,8,16,192]{3,2,1,0:T(8,128)(2,1)S(1)} %get-tuple-element.66, ...), dimensions={3} | concatenate | bytes 3538944 | tf_op jit(solution)/shard_map/concatenate | solution.py:33
  24.6 0.8 %fusion.27 = f32[512,192]{0,1:T(8,128)S(1)} fusion(bf16[512,1728]{1,0:T(8,128)(2,1)S(1)} %bitcast.30, bf16[1728,192]{1,0:T(8,128)(2,1)S(1)} %bitcast.33), kind=kOutput, calls=%fused_computation.53 | convolution fusion | flops 339738624 | bytes 2826240 | tf_op jit(solution)/shard_map/dot_general | solution.py:47
  25.3 0.0 copy-start.3
  25.3 2.9 %concatenate.55 = bf16[4,8,16,1728]{3,2,1,0:T(8,128)(2,1)S(1)} concatenate(bf16[4,8,16,192]{3,2,1,0:T(8,128)(2,1)} %get-tuple-element.40, bf16[4,8,16,192]{3,2,1,0:T(8,128)(2,1)} %get-tuple-element.72, bf16[4,8,16,192]{3,2,1,0:T(8,128)(2,1)} %get-tuple-element.39, bf16[4,8,16,192]{3,2,1,0:T(8,128)(2,1)} %get-tuple-element.38, bf16[4,8,16,192]{3,2,1,0:T(8,128)(2,1)} %get-tuple-element.65, ...), dimensions={3} | concatenate | bytes 3538944 | tf_op jit(solution)/shard_map/concatenate | solution.py:33
  28.3 0.0 copy-done.3
  28.3 1.5 %convolution_add_fusion.3 = f32[512,192]{0,1:T(8,128)} fusion(f32[512,192]{0,1:T(8,128)S(1)} %fusion.27, bf16[512,1728]{1,0:T(8,128)(2,1)S(1)} %bitcast.28, bf16[1728,192]{1,0:T(8,128)(2,1)S(1)} %bitcast.37), kind=kOutput, calls=%fused_computation.6 | convolution fusion | flops 339836928 | bytes 3219456 | tf_op jit(solution)/shard_map/dot_general | solution.py:47
  29.8 2.9 %concatenate.56 = bf16[4,8,16,1728]{3,2,1,0:T(8,128)(2,1)S(1)} concatenate(bf16[4,8,16,192]{3,2,1,0:T(8,128)(2,1)} %get-tuple-element.34, bf16[4,8,16,192]{3,2,1,0:T(8,128)(2,1)} %get-tuple-element.73, bf16[4,8,16,192]{3,2,1,0:T(8,128)(2,1)} %get-tuple-element.33, bf16[4,8,16,192]{3,2,1,0:T(8,128)(2,1)} %get-tuple-element.32, bf16[4,8,16,192]{3,2,1,0:T(8,128)(2,1)S(1)} %fusion.14, ...), dimensions={3} | concatenate | bytes 3538944 | tf_op jit(solution)/shard_map/concatenate | solution.py:33
  32.7 0.0 copy-done.1
  32.7 0.0 copy-start.4
  32.7 1.8 %convolution_add_fusion.2 = f32[512,192]{0,1:T(8,128)S(1)} fusion(f32[512,192]{0,1:T(8,128)} %convolution_add_fusion.3, bf16[512,1728]{1,0:T(8,128)(2,1)S(1)} %bitcast.26, bf16[1728,192]{1,0:T(8,128)(2,1)S(1)} %bitcast.35), kind=kOutput, calls=%fused_computation.5 | convolution fusion | flops 339836928 | bytes 3219456 | tf_op jit(solution)/shard_map/dot_general | solution.py:47
  34.5 0.2 copy.8
  34.7 0.1 multiply_convert_fusion
  34.9 3.7 %collective-permute-start.3 = (bf16[2,8,16,192]{3,2,1,0:T(8,128)(2,1)S(1)}, bf16[2,8,16,192]{3,2,1,0:T(8,128)(2,1)S(1)}, u32[]{:S(2)}, u32[]{:S(2)}) collective-permute-start(bf16[2,8,16,192]{3,2,1,0:T(8,128)(2,1)S(1)} %slice.321), channel_id=1, source_target_pairs={{0,4},{4,8},{8,12},{1,5},{5,9},{9,13},{2,6},{6,10},{10,14},{3,7},{... | collective-permute-start | bytes 294920 | tf_op jit(solution)/shard_map/ppermute | solution.py:10
  38.5 3.2 %fusion.19 = (bf16[1,3,3,192,192]{4,3,2,1,0:T(8,128)(2,1)}, bf16[1,3,3,192,192]{4,3,2,1,0:T(8,128)(2,1)S(1)}, bf16[1,3,3,192,192]{4,3,2,1,0:T(8,128)(2,1)}) fusion(bf16[3,3,3,192,192]{4,3,2,1,0:T(8,128)(2,1)} %param.8), kind=kLoop, calls=%fused_computation.45 | loop fusion | bytes 3981312 | tf_op jit(solution)/shard_map/slice | solution.py:46
  41.7 0.0 collective-permute-done.3
  41.7 2.2 %collective-permute-start.4 = (bf16[6,1,16,192]{3,2,1,0:T(8,128)(2,1)S(1)}, bf16[6,1,16,192]{3,2,1,0:T(8,128)(2,1)S(1)}, u32[]{:S(2)}, u32[]{:S(2)}) collective-permute-start(bf16[6,1,16,192]{3,2,1,0:T(8,128)(2,1)S(1)} %get-tuple-element.63), channel_id=1, source_target_pairs={{0,1},{1,2},{2,3},{4,5},{5,6},{6,7},{8,9},{9,10},{10,11},{12,13},{... | collective-permute-start | bytes 110600 | tf_op jit(solution)/shard_map/ppermute | solution.py:20
  43.9 2.2 %collective-permute-start.5 = (bf16[6,1,16,192]{3,2,1,0:T(8,128)(2,1)S(1)}, bf16[6,1,16,192]{3,2,1,0:T(8,128)(2,1)S(1)}, u32[]{:S(2)}, u32[]{:S(2)}) collective-permute-start(bf16[6,1,16,192]{3,2,1,0:T(8,128)(2,1)S(1)} %get-tuple-element.64), channel_id=1, source_target_pairs={{1,0},{2,1},{3,2},{5,4},{6,5},{7,6},{9,8},{10,9},{11,10},{13,12},{... | collective-permute-start | bytes 110600 | tf_op jit(solution)/shard_map/ppermute | solution.py:21
  46.1 0.8 %pad_maximum_fusion.2 = (bf16[4,8,16,192]{3,2,1,0:T(8,128)(2,1)}, bf16[4,8,16,192]{3,2,1,0:T(8,128)(2,1)S(1)}) fusion(bf16[4,8,16,192]{3,2,1,0:T(8,128)(2,1)S(1)} %multiply_convert_fusion, bf16[2,8,16,192]{3,2,1,0:T(8,128)(2,1)S(1)} %collective-permute-done.3), kind=kLoop, calls=%fused_computation.39 | loop fusion | flops 196608 | bytes 688128 | tf_op jit(solution)/shard_map/concatenate | solution.py:58
  46.9 0.0 collective-permute-done.4
  46.9 2.5 %collective-permute-done.5 = bf16[6,1,16,192]{3,2,1,0:T(8,128)(2,1)S(1)} collective-permute-done((bf16[6,1,16,192]{3,2,1,0:T(8,128)(2,1)S(1)}, bf16[6,1,16,192]{3,2,1,0:T(8,128)(2,1)S(1)}, u32[]{:S(2)}, u32[]{:S(2)}) %collective-permute-start.5) | collective-permute-done | bytes 36896 | tf_op jit(solution)/shard_map/ppermute | solution.py:21
  49.3 0.2 pad_maximum_fusion.1
  49.5 1.0 %fusion.23 = (bf16[4,8,16,192]{3,2,1,0:T(8,128)(2,1)}, bf16[4,8,16,192]{3,2,1,0:T(8,128)(2,1)}, bf16[4,8,16,192]{3,2,1,0:T(8,128)(2,1)}) fusion(bf16[6,9,16,192]{3,2,1,0:T(8,128)(2,1)S(1)} %get-tuple-element.61), kind=kLoop, calls=%fused_computation.49 | loop fusion | bytes 1179648 | tf_op jit(solution)/shard_map/slice | solution.py:35
  50.5 0.9 %fusion.24 = (bf16[4,8,16,192]{3,2,1,0:T(8,128)(2,1)}, bf16[4,8,16,192]{3,2,1,0:T(8,128)(2,1)}, bf16[4,8,16,192]{3,2,1,0:T(8,128)(2,1)}) fusion(bf16[6,9,16,192]{3,2,1,0:T(8,128)(2,1)S(1)} %get-tuple-element.62), kind=kLoop, calls=%fused_computation.50 | loop fusion | bytes 1179648 | tf_op jit(solution)/shard_map/slice | solution.py:35
  51.4 0.4 select_maximum_fusion
  51.8 2.2 %fusion.21 = (bf16[4,8,16,192]{3,2,1,0:T(8,128)(2,1)}, bf16[4,8,16,192]{3,2,1,0:T(8,128)(2,1)}, bf16[4,8,16,192]{3,2,1,0:T(8,128)(2,1)}, bf16[4,8,16,192]{3,2,1,...) fusion(bf16[6,10,18,192]{3,2,1,0:T(8,128)(2,1)S(1)} %select_max, ...), kind=kLoop, calls=%fused_computation.47 | loop fusion | bytes 7077888 | tf_op jit(solution)/shard_map/slice | solution.py:35
  54.0 2.8 %concatenate.61 = bf16[4,8,16,1728]{3,2,1,0:T(8,128)(2,1)S(1)} concatenate(bf16[4,8,16,192]{3,2,1,0:T(8,128)(2,1)} %get-tuple-element.28, bf16[4,8,16,192]{3,2,1,0:T(8,128)(2,1)} %get-tuple-element.52, bf16[4,8,16,192]{3,2,1,0:T(8,128)(2,1)} %get-tuple-element.27, bf16[4,8,16,192]{3,2,1,0:T(8,128)(2,1)} %get-tuple-element.26, bf16[4,8,16,192]{3,2,1,0:T(8,128)(2,1)S(1)} %get-tuple-element.60, ...), dimensions={3} | concatenate | bytes 3538944 | tf_op jit(solution)/shard_map/concatenate | solution.py:33
  56.8 0.7 %fusion.28 = f32[512,192]{0,1:T(8,128)S(1)} fusion(bf16[512,1728]{1,0:T(8,128)(2,1)S(1)} %bitcast.31, bf16[1728,192]{1,0:T(8,128)(2,1)S(1)} %bitcast.32), kind=kOutput, calls=%fused_computation.54 | convolution fusion | flops 339738624 | bytes 2826240 | tf_op jit(solution)/shard_map/dot_general | solution.py:47
  57.6 2.9 %concatenate.62 = bf16[4,8,16,1728]{3,2,1,0:T(8,128)(2,1)S(1)} concatenate(bf16[4,8,16,192]{3,2,1,0:T(8,128)(2,1)} %get-tuple-element.22, bf16[4,8,16,192]{3,2,1,0:T(8,128)(2,1)} %get-tuple-element.51, bf16[4,8,16,192]{3,2,1,0:T(8,128)(2,1)} %get-tuple-element.21, bf16[4,8,16,192]{3,2,1,0:T(8,128)(2,1)} %get-tuple-element.20, bf16[4,8,16,192]{3,2,1,0:T(8,128)(2,1)} %get-tuple-element.59, ...), dimensions={3} | concatenate | bytes 3538944 | tf_op jit(solution)/shard_map/concatenate | solution.py:33
  60.6 1.5 %convolution_add_fusion.1 = f32[512,192]{0,1:T(8,128)} fusion(f32[512,192]{0,1:T(8,128)S(1)} %fusion.28, bf16[512,1728]{1,0:T(8,128)(2,1)S(1)} %bitcast.29, bf16[1728,192]{1,0:T(8,128)(2,1)S(1)} %bitcast.36), kind=kOutput, calls=%fused_computation.4 | convolution fusion | flops 339836928 | bytes 3219456 | tf_op jit(solution)/shard_map/dot_general | solution.py:47
  62.1 2.9 %concatenate.63 = bf16[4,8,16,1728]{3,2,1,0:T(8,128)(2,1)S(1)} concatenate(bf16[4,8,16,192]{3,2,1,0:T(8,128)(2,1)} %get-tuple-element.16, bf16[4,8,16,192]{3,2,1,0:T(8,128)(2,1)} %get-tuple-element.50, bf16[4,8,16,192]{3,2,1,0:T(8,128)(2,1)} %get-tuple-element.15, bf16[4,8,16,192]{3,2,1,0:T(8,128)(2,1)} %get-tuple-element.14, bf16[4,8,16,192]{3,2,1,0:T(8,128)(2,1)S(1)} %multiply_convert_fusion, ...), dimensions={3} | concatenate | bytes 3538944 | tf_op jit(solution)/shard_map/concatenate | solution.py:33
  65.0 0.0 copy-start.5
  65.0 1.8 %convolution_add_fusion = f32[512,192]{0,1:T(8,128)S(1)} fusion(f32[512,192]{0,1:T(8,128)} %convolution_add_fusion.1, bf16[512,1728]{1,0:T(8,128)(2,1)S(1)} %bitcast.27, bf16[1728,192]{1,0:T(8,128)(2,1)S(1)} %bitcast.34), kind=kOutput, calls=%fused_computation.3 | convolution fusion | flops 339836928 | bytes 3219456 | tf_op jit(solution)/shard_map/dot_general | solution.py:47
  66.7 0.2 copy.9
  66.9 0.0 copy-done.5
  66.9 1.7 %fusion.16 = bf16[4,8,16,192]{3,2,1,0:T(8,128)(2,1)} fusion(f32[4,8,16,192]{3,2,1,0:T(8,128)S(1)} %bitcast.39, bf16[4,8,16,192]{3,2,1,0:T(8,128)(2,1)} %param.5, f32[192]{0:T(256)S(1)} %copy-done.5), kind=kLoop, calls=%fused_computation.27 | loop fusion | flops 393216 | bytes 787200 | tf_op jit(solution)/shard_map/convert_element_type | solution.py:68
  (10 shorter events, 0.1 us)
Async XLA Ops:
  1.1 7.2 %collective-permute-start = (bf16[2,8,16,192]{3,2,1,0:T(8,128)(2,1)S(1)}, bf16[2,8,16,192]{3,2,1,0:T(8,128)(2,1)S(1)}, u32[]{:S(2)}, u32[]{:S(2)}) collective-permute-start(bf16[2,8,16,192]{3,2,1,0:T(8,128)(2,1)S(1)} %slice.294), channel_id=1, source_target_pairs={{0,4},{4,8},{8,12},{1,5},{5,9},{9,13},{2,6},{6,10},{10,14},{3,7},{... | collective-permute-start | bytes 294920 | tf_op jit(solution)/shard_map/ppermute | solution.py:10
  8.4 6.7 %collective-permute-start.1 = (bf16[6,1,16,192]{3,2,1,0:T(8,128)(2,1)S(1)}, bf16[6,1,16,192]{3,2,1,0:T(8,128)(2,1)S(1)}, u32[]{:S(2)}, u32[]{:S(2)}) collective-permute-start(bf16[6,1,16,192]{3,2,1,0:T(8,128)(2,1)S(1)} %get-tuple-element.69), channel_id=1, source_target_pairs={{0,1},{1,2},{2,3},{4,5},{5,6},{6,7},{8,9},{9,10},{10,11},{12,13},{... | collective-permute-start | bytes 110600 | tf_op jit(solution)/shard_map/ppermute | solution.py:20
  12.3 5.4 %collective-permute-start.2 = (bf16[6,1,16,192]{3,2,1,0:T(8,128)(2,1)S(1)}, bf16[6,1,16,192]{3,2,1,0:T(8,128)(2,1)S(1)}, u32[]{:S(2)}, u32[]{:S(2)}) collective-permute-start(bf16[6,1,16,192]{3,2,1,0:T(8,128)(2,1)S(1)} %get-tuple-element.70), channel_id=1, source_target_pairs={{1,0},{2,1},{3,2},{5,4},{6,5},{7,6},{9,8},{10,9},{11,10},{13,12},{... | collective-permute-start | bytes 110600 | tf_op jit(solution)/shard_map/ppermute | solution.py:21
  25.3 3.0 %copy-start.3 = (bf16[1,3,3,192,192]{4,3,2,1,0:T(8,128)(2,1)S(1)}, bf16[1,3,3,192,192]{4,3,2,1,0:T(8,128)(2,1)}, u32[]{:S(2)}) copy-start(bf16[1,3,3,192,192]{4,3,2,1,0:T(8,128)(2,1)} %get-tuple-element.10) | copy-start | bytes 1990660
  29.8 2.9 %copy-start.1 = (bf16[1,3,3,192,192]{4,3,2,1,0:T(8,128)(2,1)S(1)}, bf16[1,3,3,192,192]{4,3,2,1,0:T(8,128)(2,1)}, u32[]{:S(2)}) copy-start(bf16[1,3,3,192,192]{4,3,2,1,0:T(8,128)(2,1)} %get-tuple-element.8) | copy-start | bytes 1990660
  32.7 2.0 %copy-start.4 = (f32[192]{0:T(256)S(1)}, f32[192]{0:T(256)}, u32[]{:S(2)}) copy-start(f32[192]{0:T(256)} %param.7) | copy-start | bytes 2308
  34.9 6.8 %collective-permute-start.3 = (bf16[2,8,16,192]{3,2,1,0:T(8,128)(2,1)S(1)}, bf16[2,8,16,192]{3,2,1,0:T(8,128)(2,1)S(1)}, u32[]{:S(2)}, u32[]{:S(2)}) collective-permute-start(bf16[2,8,16,192]{3,2,1,0:T(8,128)(2,1)S(1)} %slice.321), channel_id=1, source_target_pairs={{0,4},{4,8},{8,12},{1,5},{5,9},{9,13},{2,6},{6,10},{10,14},{3,7},{... | collective-permute-start | bytes 294920 | tf_op jit(solution)/shard_map/ppermute | solution.py:10
  41.7 5.1 %collective-permute-start.4 = (bf16[6,1,16,192]{3,2,1,0:T(8,128)(2,1)S(1)}, bf16[6,1,16,192]{3,2,1,0:T(8,128)(2,1)S(1)}, u32[]{:S(2)}, u32[]{:S(2)}) collective-permute-start(bf16[6,1,16,192]{3,2,1,0:T(8,128)(2,1)S(1)} %get-tuple-element.63), channel_id=1, source_target_pairs={{0,1},{1,2},{2,3},{4,5},{5,6},{6,7},{8,9},{9,10},{10,11},{12,13},{... | collective-permute-start | bytes 110600 | tf_op jit(solution)/shard_map/ppermute | solution.py:20
  43.9 5.4 %collective-permute-start.5 = (bf16[6,1,16,192]{3,2,1,0:T(8,128)(2,1)S(1)}, bf16[6,1,16,192]{3,2,1,0:T(8,128)(2,1)S(1)}, u32[]{:S(2)}, u32[]{:S(2)}) collective-permute-start(bf16[6,1,16,192]{3,2,1,0:T(8,128)(2,1)S(1)} %get-tuple-element.64), channel_id=1, source_target_pairs={{1,0},{2,1},{3,2},{5,4},{6,5},{7,6},{9,8},{10,9},{11,10},{13,12},{... | collective-permute-start | bytes 110600 | tf_op jit(solution)/shard_map/ppermute | solution.py:21
  57.6 3.0 %copy-start.2 = (bf16[1,3,3,192,192]{4,3,2,1,0:T(8,128)(2,1)S(1)}, bf16[1,3,3,192,192]{4,3,2,1,0:T(8,128)(2,1)}, u32[]{:S(2)}) copy-start(bf16[1,3,3,192,192]{4,3,2,1,0:T(8,128)(2,1)} %get-tuple-element.7) | copy-start | bytes 1990660
  62.1 2.9 %copy-start = (bf16[1,3,3,192,192]{4,3,2,1,0:T(8,128)(2,1)S(1)}, bf16[1,3,3,192,192]{4,3,2,1,0:T(8,128)(2,1)}, u32[]{:S(2)}) copy-start(bf16[1,3,3,192,192]{4,3,2,1,0:T(8,128)(2,1)} %get-tuple-element.5) | copy-start | bytes 1990660
  65.0 2.0 %copy-start.5 = (f32[192]{0:T(256)S(1)}, f32[192]{0:T(256)}, u32[]{:S(2)}) copy-start(f32[192]{0:T(256)} %param.9) | copy-start | bytes 2308
where the time goes:
time: 69.7 us; the launch traced here: 68.7 us
  local copies, waits for them, and re-layouts  31.6 us (45%)
  starting transfers between devices  17.9 us (26%)
  matrix products  8.06 us (12%)
  other arithmetic  5.74 us (8%)
  waiting for transfers between devices  5.15 us (7%)
    concatenate x6, local copies, waits for them, and re-layouts, conv_valid(): jnp.concatenate([padded[tap_time:tap_time + frame_count, tap_row:tap_row...  17.2 us
    dot_general x6, matrix products, conv_valid(): jnp.dot(stacked, kernel, preferred_element_type=jnp.float32)  8.06 us
    ppermute x2, starting transfers between devices, shifted(): lax.ppermute(value, axis, [(source, source + steps) for source in range(l...  7.7 us
    slice x5, local copies, waits for them, and re-layouts, conv_valid(): padded[tap_time:tap_time + frame_count, tap_row:tap_row + row_count, tap_...  7.59 us
    slice x2, local copies, waits for them, and re-layouts, conv_valid(): kernel = weight[tap_time].reshape(9 * chans, weight.shape[4])  6.35 us
    ppermute x2, starting transfers between devices, with_halo(): before = lax.ppermute(last, axis, up)  6.13 us
    ppermute x2, waiting for transfers between devices, with_halo(): after = lax.ppermute(leading, axis, down)  5.14 us
    ppermute x2, starting transfers between devices, with_halo(): after = lax.ppermute(leading, axis, down)  4.07 us
  transfers between devices with their start and end apart: 6, of which 2 were waited for; matrix products, arithmetic and copies ran while one was open for 12% of the time, Pallas kernels for 0%

commit v1 on v0

v1 whole, which is shorter than its diff:
```python
import functools

import jax
import jax.numpy as jnp
from jax import lax
from jax.experimental import pallas as pl
from jax.experimental.pallas import tpu as pltpu
from jax.sharding import PartitionSpec as P

MESH = pl.DeviceIdType.MESH


def silu(v):
    return 0.5 * v * (1.0 + jnp.tanh(0.5 * v))


def kernel(
    peers_t, peers_h, x_ref, w1_ref, b1_ref, w2_ref, b2_ref, out_ref,
    xbuf, gbuf, stack1, stack2, wv1, wv2, bias, x_sem, b_sem, w_sem, send_sem, recv_sem,
):
    frames, rows, cols, chans = x_ref.shape
    lo_chans = chans - 128
    positions = frames * rows * cols
    depth = stack1.shape[-1]
    tm, height = lax.axis_index("tm"), lax.axis_index("height")
    later, lower, upper = tm < peers_t - 1, height < peers_h - 1, height > 0
    earlier = tm > 0

    every, tail, head = slice(0, frames), slice(frames - 2, frames), slice(0, 2)
    body, first, last = slice(0, rows), slice(0, 1), slice(rows - 1, rows)
    own_f, own_r = slice(2, frames + 2), slice(1, rows + 1)
    above, below = slice(0, 1), slice(rows + 1, rows + 2)
    routes = (
        (1, 0, tail, body, head, own_r, later, earlier),
        (0, 1, every, last, own_f, above, lower, upper),
        (0, -1, every, first, own_f, below, upper, lower),
        (1, 1, tail, last, head, above, later & lower, earlier & upper),
        (1, -1, tail, first, head, below, later & upper, earlier & lower),
    )

    barrier = pltpu.get_barrier_semaphore()
    for dt, dh, _, _, _, _, _, receives in routes:
        @pl.when(receives)
        def _():
            pl.semaphore_signal(
                barrier, inc=1,
                device_id={"tm": jnp.maximum(tm - dt, 0), "height": jnp.clip(height - dh, 0, peers_h - 1)},
                device_id_type=MESH,
            )

    local_x = pltpu.make_async_copy(x_ref, xbuf.at[own_f, own_r], x_sem)
    local_x.start()

    def weight_copies(w_ref, b_ref, wv, which):
        copies = [pltpu.make_async_copy(b_ref, bias.at[which], b_sem.at[which])]
        for a in range(3):
            pairs = [(w_ref.at[a, b, :, 0:2], wv.at[a, 3 * b : 3 * b + 3]) for b in range(3)]
            pairs.append((w_ref.at[a, :, 0:2, 2], wv.at[a, 9:12]))
            pairs.append((w_ref.at[a, 0:2, 2, 2], wv.at[a, 12]))
            pairs.append((w_ref.at[a, 2, 2, 2], wv.at[a, 13, 0]))
            for n, (src, dst) in enumerate(pairs):
                copies.append(pltpu.make_async_copy(src, dst, w_sem.at[which, a, n]))
        return copies

    w1_copies, w2_copies = weight_copies(w1_ref, b1_ref, wv1, 0), weight_copies(w2_ref, b2_ref, wv2, 1)
    for copy in w1_copies:
        copy.start()
    for copy in w2_copies:
        copy.start()

    def exchange(src, src_f, src_r, dst, stage):
        made = []
        for n, (dt, dh, f, r, to_f, to_r, sends, receives) in enumerate(routes):
            f = slice(f.start + src_f, f.stop + src_f)
            r = slice(r.start + src_r, r.stop + src_r)
            copy = pltpu.make_async_remote_copy(
                src_ref=src.at[f, r],
                dst_ref=dst.at[to_f, to_r],
                send_sem=send_sem.at[stage, n],
                recv_sem=recv_sem.at[stage, n],
                device_id={"tm": jnp.minimum(tm + dt, peers_t - 1), "height": jnp.clip(height + dh, 0, peers_h - 1)},
                device_id_type=MESH,
            )
            made.append((copy, sends, receives))
        return made

    def start(made):
        for copy, sends, _ in made:
            pl.when(sends)(copy.start)

    def finish(made, which):
        for copy, sends, receives in made:
            if which == "recv":
                pl.when(receives)(copy.wait_recv)
            else:
                pl.when(sends)(copy.wait_send)

    pl.semaphore_wait(barrier, sum(sends.astype(jnp.int32) for _, _, _, _, _, _, sends, _ in routes))

    sent_x = exchange(x_ref, 0, 0, xbuf, 0)
    start(sent_x)

    for buf in (xbuf, gbuf):
        @pl.when(jnp.logical_not(earlier))
        def _():
            buf[0:2] = jnp.zeros((2, rows + 2, cols, chans), buf.dtype)

        @pl.when(jnp.logical_not(upper))
        def _():
            buf[:, 0:1] = jnp.zeros((frames + 2, 1, cols, chans), buf.dtype)

        @pl.when(jnp.logical_not(lower))
        def _():
            buf[:, rows + 1 : rows + 2] = jnp.zeros((frames + 2, 1, cols, chans), buf.dtype)

    for wv in (wv1, wv2):
        for a in range(3):
            wv[a, 13, 1] = jnp.zeros((lo_chans, chans), wv.dtype)

    def lay(stack, value, f0, r0):
        nf, nr = value.shape[:2]
        column = lax.broadcasted_iota(jnp.int32, value.shape, 2)
        turned = (
            jnp.where(column == 0, 0.0, pltpu.roll(value, 1, 2)),
            value,
            jnp.where(column == cols - 1, 0.0, pltpu.roll(value, cols - 1, 2)),
        )
        high = [v[..., :128].astype(stack.dtype) for v in turned]
        low = [v[..., 128:] for v in turned]
        low01 = jnp.concatenate([low[0], low[1]], -1).astype(stack.dtype)
        low2 = jnp.concatenate([low[2], jnp.zeros_like(low[2])], -1).astype(stack.dtype)
        low2_right = jnp.concatenate([jnp.zeros_like(low[2]), low[2]], -1).astype(stack.dtype)
        for b in range(3):
            begin, end = max(r0 - b, 0), min(r0 + nr - b, rows)
            if begin >= end:
                continue
            source = slice(begin + b - r0, end + b - r0)
            target = (slice(f0, f0 + nf), slice(begin, end), slice(None))
            for e in range(3):
                stack[target + (slice((3 * b + e) * 128, (3 * b + e + 1) * 128),)] = high[e][:, source]
            stack[target + (slice(1152 + b * 128, 1280 + b * 128),)] = low01[:, source]
            if b == 0:
                stack[target + (slice(1536, 1536 + lo_chans),)] = low2[:, source][..., :lo_chans]
            elif b == 1:
                stack[target + (slice(1536 + lo_chans, 1664),)] = low2_right[:, source][..., lo_chans:]
            else:
                stack[target + (slice(1664, 1792),)] = low2[:, source]

    def lay_halo(stack, buf, fn):
        for f in range(2):
            lay(stack, fn(buf[f : f + 1].astype(jnp.float32)), f, 0)
        lay(stack, fn(buf[2 : frames + 2, 0:1].astype(jnp.float32)), 2, 0)
        lay(stack, fn(buf[2 : frames + 2, rows + 1 : rows + 2].astype(jnp.float32)), 2, rows + 1)

    def conv(stack, wv):
        left = jnp.concatenate([stack[a : a + frames].reshape(positions, depth) for a in range(3)], -1)
        return jnp.dot(left, wv[...].reshape(3 * depth, chans), preferred_element_type=jnp.float32)

    local_x.wait()
    for f in range(2, frames + 2):
        lay(stack1, silu(xbuf[f : f + 1, 1 : rows + 1].astype(jnp.float32)), f, 1)
    finish(sent_x, "recv")
    lay_halo(stack1, xbuf, silu)
    for copy in w1_copies:
        copy.wait()
    gated = silu(conv(stack1, wv1) + bias[0]).astype(jnp.bfloat16)
    gbuf[2 : frames + 2, 1 : rows + 1] = gated.reshape(frames, rows, cols, chans)

    sent_g = exchange(gbuf, 2, 1, gbuf, 1)
    start(sent_g)
    for f in range(2, frames + 2):
        lay(stack2, gbuf[f : f + 1, 1 : rows + 1].astype(jnp.float32), f, 1)
    for copy in w2_copies:
        copy.wait()
    finish(sent_g, "recv")
    lay_halo(stack2, gbuf, lambda v: v)
    total = conv(stack2, wv2) + bias[1]
    own = xbuf[2 : frames + 2, 1 : rows + 1].astype(jnp.float32)
    out_ref[...] = (own + total.reshape(frames, rows, cols, chans)).astype(out_ref.dtype)
    finish(sent_x, "send")
    finish(sent_g, "send")


def local(peers_t, peers_h, clip_frames, w_first, b_first, w_second, b_second):
    frames, rows, cols, chans = clip_frames.shape
    kind = clip_frames.dtype
    parts = chans // 64
    padded = (frames + 2, rows + 2, cols, chans)
    stacked = (frames + 2, rows, cols, 14 * 128)
    weights = (3, 14, 2, 64, chans)
    anywhere, vmem = pl.BlockSpec(memory_space=pltpu.HBM), pl.BlockSpec(memory_space=pltpu.VMEM)
    return pl.pallas_call(
        functools.partial(kernel, peers_t, peers_h),
        out_shape=jax.ShapeDtypeStruct(clip_frames.shape, kind),
        in_specs=[anywhere] * 5,
        out_specs=vmem,
        scratch_shapes=[
            pltpu.VMEM(padded, kind),
            pltpu.VMEM(padded, kind),
            pltpu.VMEM(stacked, kind),
            pltpu.VMEM(stacked, kind),
            pltpu.VMEM(weights, kind),
            pltpu.VMEM(weights, kind),
            pltpu.VMEM((2, 1, chans), jnp.float32),
            pltpu.SemaphoreType.DMA,
            pltpu.SemaphoreType.DMA((2,)),
            pltpu.SemaphoreType.DMA((2, 3, 6)),
            pltpu.SemaphoreType.DMA((2, 5)),
            pltpu.SemaphoreType.DMA((2, 5)),
        ],
        compiler_params=pltpu.CompilerParams(
            collective_id=0, has_side_effects=True, vmem_limit_bytes=61 * 1024 * 1024
        ),
    )(
        clip_frames,
        w_first.reshape(3, 3, 3, parts, 64, chans),
        b_first.reshape(1, chans),
        w_second.reshape(3, 3, 3, parts, 64, chans),
        b_second.reshape(1, chans),
    )


def solution(mesh):
    return jax.shard_map(
        functools.partial(local, mesh.shape["tm"], mesh.shape["height"]),
        mesh=mesh,
        in_specs=(P(("clips", "tm"), "height", None, None), P(), P(), P(), P()),
        out_specs=P(("clips", "tm"), "height", None, None),
        check_vma=False,
    )
```

time: 69.7 us -> 21.4 us (0.31)
  the two profiles are of different devices: /device:TPU:1 before, /device:TPU:17 now
where the time goes in v1:
time: 21.4 us; the launch traced here: 21.2 us
  Pallas kernels  19.6 us (92%)
  local copies, waits for them, and re-layouts  1.67 us (8%)
    pallas_call x1, Pallas kernels, local(): pl.pallas_call(functools.partial(kernel, peers_t, peers_h), out_shape=jax...  19.6 us
    unnamed x1, local copies, waits for them, and re-layouts  1.67 us

profile of v1, /device:TPU:17, one launch (start us, length us, event | category | flops | bytes accessed | tf_op | source)
XLA Modules:
  0.0 21.2 jit_solution(2307920123958837725)
XLA Ops:
  0.0 19.6 %shard_map.55 = bf16[4,8,16,192]{3,2,1,0:T(8,128)(2,1)} custom-call(bf16[4,8,16,192]{3,2,1,0:T(8,128)(2,1)} %x_ref.1, bf16[3,3,3,3,64,192]{5,4,3,2,1,0:T(8,128)(2,1)} %bitcast.4, f32[1,192]{1,0:T(1,128)} %bitcast.6, bf16[3,3,3,3,64,192]{5,4,3,2,1,0:T(8,128)(2,1)} %bitcast.5, f32[1,192]{1,0:T(1,128)} %bitcast.7), custom_call_target="tpu_custom_call" | custom-call | tf_op jit(solution)/shard_map/pallas_call | solution.py:192
  19.6 1.7 %copy.7 = bf16[4,8,16,192]{3,2,1,0:T(8,128)(2,1)} copy(bf16[4,8,16,192]{3,2,1,0:T(8,128)(2,1)} %shard_map.55) | data formatting | bytes 393216

commit v2 on v1

--- a/solution.py
+++ b/solution.py
@@ -26,17 +26,23 @@
     later, lower, upper = tm < peers_t - 1, height < peers_h - 1, height > 0
     earlier = tm > 0
 
-    every, tail, head = slice(0, frames), slice(frames - 2, frames), slice(0, 2)
-    body, first, last = slice(0, rows), slice(0, 1), slice(rows - 1, rows)
-    own_f, own_r = slice(2, frames + 2), slice(1, rows + 1)
+    every, tail, before = slice(2, frames + 2), slice(frames, frames + 2), slice(0, 2)
+    body, first, last = slice(1, rows + 1), slice(1, 2), slice(rows, rows + 1)
     above, below = slice(0, 1), slice(rows + 1, rows + 2)
-    routes = (
-        (1, 0, tail, body, head, own_r, later, earlier),
-        (0, 1, every, last, own_f, above, lower, upper),
-        (0, -1, every, first, own_f, below, upper, lower),
-        (1, 1, tail, last, head, above, later & lower, earlier & upper),
-        (1, -1, tail, first, head, below, later & upper, earlier & lower),
+    own_f, own_r = every, body
+
+    def rows_of(f):
+        return (
+            (0, 1, f, last, f, above, lower, upper),
+            (0, -1, f, first, f, below, upper, lower),
+        )
+
+    onward = (
+        (1, 0, tail, body, before, body, later, earlier),
+        (1, 1, tail, last, before, above, later & lower, earlier & upper),
+        (1, -1, tail, first, before, below, later & upper, earlier & lower),
     )
+    routes = rows_of(every) + onward
 
     barrier = pltpu.get_barrier_semaphore()
     for dt, dh, _, _, _, _, _, receives in routes:
@@ -65,14 +71,11 @@
     w1_copies, w2_copies = weight_copies(w1_ref, b1_ref, wv1, 0), weight_copies(w2_ref, b2_ref, wv2, 1)
     for copy in w1_copies:
         copy.start()
-    for copy in w2_copies:
-        copy.start()
-
-    def exchange(src, src_f, src_r, dst, stage):
+    def exchange(src, base_f, base_r, dst, plan, stage, sem):
         made = []
-        for n, (dt, dh, f, r, to_f, to_r, sends, receives) in enumerate(routes):
-            f = slice(f.start + src_f, f.stop + src_f)
-            r = slice(r.start + src_r, r.stop + src_r)
+        for n, (dt, dh, f, r, to_f, to_r, sends, receives) in enumerate(plan, sem):
+            f = slice(f.start - base_f, f.stop - base_f)
+            r = slice(r.start - base_r, r.stop - base_r)
             copy = pltpu.make_async_remote_copy(
                 src_ref=src.at[f, r],
                 dst_ref=dst.at[to_f, to_r],
@@ -97,8 +100,10 @@
 
     pl.semaphore_wait(barrier, sum(sends.astype(jnp.int32) for _, _, _, _, _, _, sends, _ in routes))
 
-    sent_x = exchange(x_ref, 0, 0, xbuf, 0)
+    sent_x = exchange(x_ref, 2, 1, xbuf, routes, 0, 0)
     start(sent_x)
+    for copy in w2_copies:
+        copy.start()
 
     for buf in (xbuf, gbuf):
         @pl.when(jnp.logical_not(earlier))
@@ -146,39 +151,76 @@
             else:
                 stack[target + (slice(1664, 1792),)] = low2[:, source]
 
-    def lay_halo(stack, buf, fn):
+    def lay_rows(stack, buf, fn, f):
+        lay(stack, fn(buf[f, 0:1].astype(jnp.float32)), f.start, 0)
+        lay(stack, fn(buf[f, rows + 1 : rows + 2].astype(jnp.float32)), f.start, rows + 1)
+
+    def lay_before(stack, buf, fn):
         for f in range(2):
             lay(stack, fn(buf[f : f + 1].astype(jnp.float32)), f, 0)
-        lay(stack, fn(buf[2 : frames + 2, 0:1].astype(jnp.float32)), 2, 0)
-        lay(stack, fn(buf[2 : frames + 2, rows + 1 : rows + 2].astype(jnp.float32)), 2, rows + 1)
-
-    def conv(stack, wv):
-        left = jnp.concatenate([stack[a : a + frames].reshape(positions, depth) for a in range(3)], -1)
+
+    def conv(stack, wv, pieces):
+        left = jnp.concatenate(
+            [
+                jnp.concatenate(
+                    [
+                        stack[a + f.start : a + f.stop, r].reshape((f.stop - f.start) * (r.stop - r.start) * cols, depth)
+                        for f, r in pieces
+                    ],
+                    0,
+                )
+                for a in range(3)
+            ],
+            -1,
+        )
         return jnp.dot(left, wv[...].reshape(3 * depth, chans), preferred_element_type=jnp.float32)
+
+    def gate(f):
+        total = conv(stack1, wv1, [(f, slice(0, rows))])
+        gated = silu(total + bias[0]).astype(gbuf.dtype).reshape(f.stop - f.start, rows, cols, chans)
+        gbuf[f.start + 2 : f.stop + 2, 1 : rows + 1] = gated
+        return gated.astype(jnp.float32)
+
+    def finish_block(pieces):
+        total = conv(stack2, wv2, pieces) + bias[1]
+        begin = 0
+        for f, r in pieces:
+            nf, nr = f.stop - f.start, r.stop - r.start
+            part = total[begin : begin + nf * nr * cols].reshape(nf, nr, cols, chans)
+            begin += nf * nr * cols
+            own = xbuf[f.start + 2 : f.stop + 2, r.start + 1 : r.stop + 1].astype(jnp.float32)
+            out_ref[f, r] = (own + part).astype(out_ref.dtype)
 
     local_x.wait()
     for f in range(2, frames + 2):
         lay(stack1, silu(xbuf[f : f + 1, 1 : rows + 1].astype(jnp.float32)), f, 1)
-    finish(sent_x, "recv")
-    lay_halo(stack1, xbuf, silu)
     for copy in w1_copies:
         copy.wait()
-    gated = silu(conv(stack1, wv1) + bias[0]).astype(jnp.bfloat16)
-    gbuf[2 : frames + 2, 1 : rows + 1] = gated.reshape(frames, rows, cols, chans)
-
-    sent_g = exchange(gbuf, 2, 1, gbuf, 1)
+    finish(sent_x[:2], "recv")
+    lay_rows(stack1, xbuf, silu, every)
+
+    late, soon = slice(2, frames), slice(0, 2)
+    gated = gate(late)
+    sent_g = exchange(gbuf, 0, 0, gbuf, onward + rows_of(slice(4, frames + 2)), 1, 0)
     start(sent_g)
-    for f in range(2, frames + 2):
-        lay(stack2, gbuf[f : f + 1, 1 : rows + 1].astype(jnp.float32), f, 1)
+    lay(stack2, gated, 4, 1)
+    finish(sent_x[2:], "recv")
+    lay_before(stack1, xbuf, silu)
+    gated = gate(soon)
+    sent_rows = exchange(gbuf, 0, 0, gbuf, rows_of(slice(2, 4)), 1, 5)
+    start(sent_rows)
+    lay(stack2, gated, 2, 1)
     for copy in w2_copies:
         copy.wait()
+    finish_block([(late, slice(1, rows - 1))])
     finish(sent_g, "recv")
-    lay_halo(stack2, gbuf, lambda v: v)
-    total = conv(stack2, wv2) + bias[1]
-    own = xbuf[2 : frames + 2, 1 : rows + 1].astype(jnp.float32)
-    out_ref[...] = (own + total.reshape(frames, rows, cols, chans)).astype(out_ref.dtype)
+    finish(sent_rows, "recv")
+    lay_rows(stack2, gbuf, lambda v: v, every)
+    lay_before(stack2, gbuf, lambda v: v)
+    finish_block([(soon, slice(0, rows)), (late, slice(0, 1)), (late, slice(rows - 1, rows))])
     finish(sent_x, "send")
     finish(sent_g, "send")
+    finish(sent_rows, "send")
 
 
 def local(peers_t, peers_h, clip_frames, w_first, b_first, w_second, b_second):
@@ -205,8 +247,8 @@
             pltpu.SemaphoreType.DMA,
             pltpu.SemaphoreType.DMA((2,)),
             pltpu.SemaphoreType.DMA((2, 3, 6)),
-            pltpu.SemaphoreType.DMA((2, 5)),
-            pltpu.SemaphoreType.DMA((2, 5)),
+            pltpu.SemaphoreType.DMA((2, 7)),
+            pltpu.SemaphoreType.DMA((2, 7)),
         ],
         compiler_params=pltpu.CompilerParams(
             collective_id=0, has_side_effects=True, vmem_limit_bytes=61 * 1024 * 1024

time: 21.4 us -> 16.7 us (0.78)
  the two profiles are of different devices: /device:TPU:17 before, /device:TPU:1 now
where the time goes in v2:
time: 16.7 us; the launch traced here: 16.6 us
  Pallas kernels  14.9 us (89%)
  local copies, waits for them, and re-layouts  1.67 us (10%)
    pallas_call x1, Pallas kernels, local(): pl.pallas_call(functools.partial(kernel, peers_t, peers_h), out_shape=jax...  14.9 us
    unnamed x1, local copies, waits for them, and re-layouts  1.67 us

profile of v2, /device:TPU:1, one launch (start us, length us, event | category | flops | bytes accessed | tf_op | source)
XLA Modules:
  0.0 16.6 jit_solution(10821511701154410639)
XLA Ops:
  0.0 14.9 %shard_map.55 = bf16[4,8,16,192]{3,2,1,0:T(8,128)(2,1)} custom-call(bf16[4,8,16,192]{3,2,1,0:T(8,128)(2,1)} %x_ref.1, bf16[3,3,3,3,64,192]{5,4,3,2,1,0:T(8,128)(2,1)} %bitcast.4, f32[1,192]{1,0:T(1,128)} %bitcast.6, bf16[3,3,3,3,64,192]{5,4,3,2,1,0:T(8,128)(2,1)} %bitcast.5, f32[1,192]{1,0:T(1,128)} %bitcast.7), custom_call_target="tpu_custom_call" | custom-call | tf_op jit(solution)/shard_map/pallas_call | solution.py:234
  14.9 1.7 %copy.7 = bf16[4,8,16,192]{3,2,1,0:T(8,128)(2,1)} copy(bf16[4,8,16,192]{3,2,1,0:T(8,128)(2,1)} %shard_map.55) | data formatting | bytes 393216

commit v3 on v2

--- a/solution.py
+++ b/solution.py
@@ -175,11 +175,20 @@
         )
         return jnp.dot(left, wv[...].reshape(3 * depth, chans), preferred_element_type=jnp.float32)
 
-    def gate(f):
-        total = conv(stack1, wv1, [(f, slice(0, rows))])
-        gated = silu(total + bias[0]).astype(gbuf.dtype).reshape(f.stop - f.start, rows, cols, chans)
-        gbuf[f.start + 2 : f.stop + 2, 1 : rows + 1] = gated
-        return gated.astype(jnp.float32)
+    def gate(pieces):
+        gated = silu(conv(stack1, wv1, pieces) + bias[0]).astype(gbuf.dtype)
+        made, begin = [], 0
+        for f, r in pieces:
+            nf, nr = f.stop - f.start, r.stop - r.start
+            part = gated[begin : begin + nf * nr * cols].reshape(nf, nr, cols, chans)
+            begin += nf * nr * cols
+            gbuf[f.start + 2 : f.stop + 2, r.start + 1 : r.stop + 1] = part
+            made.append((part.astype(jnp.float32), f.start + 2, r.start + 1))
+        return made
+
+    def lay_own(made):
+        for value, f0, r0 in made:
+            lay(stack2, value, f0, r0)
 
     def finish_block(pieces):
         total = conv(stack2, wv2, pieces) + bias[1]
@@ -196,29 +205,34 @@
         lay(stack1, silu(xbuf[f : f + 1, 1 : rows + 1].astype(jnp.float32)), f, 1)
     for copy in w1_copies:
         copy.wait()
+    late, soon = slice(2, frames), slice(0, 2)
+    inner = gate([(late, slice(1, rows - 1))])
+    sent_inner = exchange(gbuf, 0, 0, gbuf, ((1, 0, tail, slice(2, rows), before, slice(2, rows), later, earlier),), 1, 0)
+    start(sent_inner)
     finish(sent_x[:2], "recv")
     lay_rows(stack1, xbuf, silu, every)
-
-    late, soon = slice(2, frames), slice(0, 2)
-    gated = gate(late)
-    sent_g = exchange(gbuf, 0, 0, gbuf, onward + rows_of(slice(4, frames + 2)), 1, 0)
+    edges = gate([(late, slice(0, 1)), (late, slice(rows - 1, rows))])
+    edge_routes = tuple((1, 0, tail, r, before, r, later, earlier) for r in (first, last))
+    sent_g = exchange(gbuf, 0, 0, gbuf, edge_routes + onward[1:] + rows_of(slice(4, frames + 2)), 1, 1)
     start(sent_g)
-    lay(stack2, gated, 4, 1)
+    lay_own(inner + edges)
     finish(sent_x[2:], "recv")
     lay_before(stack1, xbuf, silu)
-    gated = gate(soon)
-    sent_rows = exchange(gbuf, 0, 0, gbuf, rows_of(slice(2, 4)), 1, 5)
+    gated = gate([(soon, slice(0, rows))])
+    sent_rows = exchange(gbuf, 0, 0, gbuf, rows_of(slice(2, 4)), 1, 7)
     start(sent_rows)
-    lay(stack2, gated, 2, 1)
+    lay_own(gated)
     for copy in w2_copies:
         copy.wait()
     finish_block([(late, slice(1, rows - 1))])
+    finish(sent_inner, "recv")
     finish(sent_g, "recv")
     finish(sent_rows, "recv")
     lay_rows(stack2, gbuf, lambda v: v, every)
     lay_before(stack2, gbuf, lambda v: v)
     finish_block([(soon, slice(0, rows)), (late, slice(0, 1)), (late, slice(rows - 1, rows))])
     finish(sent_x, "send")
+    finish(sent_inner, "send")
     finish(sent_g, "send")
     finish(sent_rows, "send")
 
@@ -247,8 +261,8 @@
             pltpu.SemaphoreType.DMA,
             pltpu.SemaphoreType.DMA((2,)),
             pltpu.SemaphoreType.DMA((2, 3, 6)),
-            pltpu.SemaphoreType.DMA((2, 7)),
-            pltpu.SemaphoreType.DMA((2, 7)),
+            pltpu.SemaphoreType.DMA((2, 9)),
+            pltpu.SemaphoreType.DMA((2, 9)),
         ],
         compiler_params=pltpu.CompilerParams(
             collective_id=0, has_side_effects=True, vmem_limit_bytes=61 * 1024 * 1024

time: 16.7 us -> 16.3 us (0.976)
  the two profiles are of different devices: /device:TPU:1 before, /device:TPU:17 now
where the time goes in v3:
time: 16.3 us; the launch traced here: 16.1 us
  Pallas kernels  14.5 us (89%)
  local copies, waits for them, and re-layouts  1.67 us (10%)
    pallas_call x1, Pallas kernels, local(): pl.pallas_call(functools.partial(kernel, peers_t, peers_h), out_shape=jax...  14.5 us
    unnamed x1, local copies, waits for them, and re-layouts  1.67 us

profile of v3, /device:TPU:17, one launch (start us, length us, event | category | flops | bytes accessed | tf_op | source)
XLA Modules:
  0.0 16.1 jit_solution(4024354036894573243)
XLA Ops:
  0.0 14.5 %shard_map.55 = bf16[4,8,16,192]{3,2,1,0:T(8,128)(2,1)} custom-call(bf16[4,8,16,192]{3,2,1,0:T(8,128)(2,1)} %x_ref.1, bf16[3,3,3,3,64,192]{5,4,3,2,1,0:T(8,128)(2,1)} %bitcast.4, f32[1,192]{1,0:T(1,128)} %bitcast.6, bf16[3,3,3,3,64,192]{5,4,3,2,1,0:T(8,128)(2,1)} %bitcast.5, f32[1,192]{1,0:T(1,128)} %bitcast.7), custom_call_target="tpu_custom_call" | custom-call | tf_op jit(solution)/shard_map/pallas_call | solution.py:248
  14.5 1.7 %copy.7 = bf16[4,8,16,192]{3,2,1,0:T(8,128)(2,1)} copy(bf16[4,8,16,192]{3,2,1,0:T(8,128)(2,1)} %shard_map.55) | data formatting | bytes 393216

commit v4 on v3

--- a/solution.py
+++ b/solution.py
@@ -215,13 +215,12 @@
     edge_routes = tuple((1, 0, tail, r, before, r, later, earlier) for r in (first, last))
     sent_g = exchange(gbuf, 0, 0, gbuf, edge_routes + onward[1:] + rows_of(slice(4, frames + 2)), 1, 1)
     start(sent_g)
-    lay_own(inner + edges)
     finish(sent_x[2:], "recv")
     lay_before(stack1, xbuf, silu)
     gated = gate([(soon, slice(0, rows))])
     sent_rows = exchange(gbuf, 0, 0, gbuf, rows_of(slice(2, 4)), 1, 7)
     start(sent_rows)
-    lay_own(gated)
+    lay_own(inner + edges + gated)
     for copy in w2_copies:
         copy.wait()
     finish_block([(late, slice(1, rows - 1))])

time: 16.3 us -> 16.3 us (level)
  no operation moved by 1% of the time
where the time goes in v4:
time: 16.3 us; the launch traced here: 16.1 us
  Pallas kernels  14.5 us (89%)
  local copies, waits for them, and re-layouts  1.67 us (10%)
    pallas_call x1, Pallas kernels, local(): pl.pallas_call(functools.partial(kernel, peers_t, peers_h), out_shape=jax...  14.5 us
    unnamed x1, local copies, waits for them, and re-layouts  1.67 us

profile of v4, /device:TPU:17, one launch (start us, length us, event | category | flops | bytes accessed | tf_op | source)
XLA Modules:
  0.0 16.1 jit_solution(6573000637927951670)
XLA Ops:
  0.0 14.5 %shard_map.55 = bf16[4,8,16,192]{3,2,1,0:T(8,128)(2,1)} custom-call(bf16[4,8,16,192]{3,2,1,0:T(8,128)(2,1)} %x_ref.1, bf16[3,3,3,3,64,192]{5,4,3,2,1,0:T(8,128)(2,1)} %bitcast.4, f32[1,192]{1,0:T(1,128)} %bitcast.6, bf16[3,3,3,3,64,192]{5,4,3,2,1,0:T(8,128)(2,1)} %bitcast.5, f32[1,192]{1,0:T(1,128)} %bitcast.7), custom_call_target="tpu_custom_call" | custom-call | tf_op jit(solution)/shard_map/pallas_call | solution.py:247
  14.5 1.7 %copy.7 = bf16[4,8,16,192]{3,2,1,0:T(8,128)(2,1)} copy(bf16[4,8,16,192]{3,2,1,0:T(8,128)(2,1)} %shard_map.55) | data formatting | bytes 393216
